TPU v7x, 32 devices: a whole 2x2x4 slice. The times are simulated.
32 devices in a mesh: blk: 8 (over y, x, core), off: 4 (over z).
Axes of the slice: x: 2, y: 2, z: 4, core: 2. Of those that a mesh axis runs over, the one named last changes fastest.
Arguments:
- coefficients: bfloat16 [128, 32, 128], P('blk', 'off'), may hold values from -12 to 12
Outputs:
- smoothed: float32 [128, 32, 128], P(('blk', 'off'))
- log_degree: float32 [128], P(('blk', 'off'))
All inputs are finite; a program needn't handle non-finite values.
Results may differ from a plain program's by a relative error of at most 0.005.
Values may be sent and summed in bfloat16 or wider, within the bound.
No kernel may reach another device: no remote copies, remote signals or barrier semaphores. Data moves between devices by JAX's collectives and lax.ppermute only.
A program may use at most 64 MiB of HBM per device.

v0:
```python
import math
import jax
import jax.numpy as jnp
from jax import lax
from jax.sharding import PartitionSpec as P

epsilon = 1e-06
concentration = 40.0


def shifted(array, axis, by):
    count = lax.axis_size(axis)
    return lax.ppermute(array, axis, [(i, (i + by) % count) for i in range(count)])


def angle_tables(angular):
    half_width = angular // 2
    frequency = jnp.arange(half_width, dtype=jnp.int32)
    shifts = jnp.arange(angular, dtype=jnp.int32)
    product = frequency[:, None] * shifts[None, :] % angular
    phase = product.astype(jnp.float32) * (2.0 * math.pi / angular)
    forward = jnp.concatenate([jnp.cos(phase), -jnp.sin(phase)], axis=0)
    return (forward, forward.T)


def inverse_norms(block_values):
    values = block_values.astype(jnp.float32)
    return lax.rsqrt(jnp.sum(values * values, axis=(1, 2)) + epsilon)


def tile_terms(own_block, own_inverse, other_block, offset, forward, backward):
    row_count = own_block.shape[0]
    half_width = own_block.shape[2] // 2
    highest = lax.Precision.HIGHEST
    other_inverse = inverse_norms(other_block)
    swapped = jnp.concatenate(
        [other_block[:, :, half_width:], other_block[:, :, :half_width]], axis=2
    )
    direct = jnp.einsum("irc,jrc->ijc", own_block, other_block, preferred_element_type=jnp.float32)
    mixed_terms = jnp.einsum("irc,jrc->ijc", own_block, swapped, preferred_element_type=jnp.float32)
    real_part = direct[:, :, :half_width] + direct[:, :, half_width:]
    imag_part = mixed_terms[:, :, half_width:] - mixed_terms[:, :, :half_width]
    cross_spectrum = jnp.concatenate([real_part, imag_part], axis=2).reshape(
        row_count * row_count, -1
    )
    correlation = jnp.dot(
        cross_spectrum, forward, precision=highest, preferred_element_type=jnp.float32
    )
    correlation = correlation.reshape(row_count, row_count, -1)
    cosine = correlation * own_inverse[:, None, None] * other_inverse[None, :, None]
    same_image = jnp.arange(row_count)[:, None] == jnp.arange(row_count)[None, :]
    keep_mask = jnp.where(jnp.logical_and(offset == 0, same_image), 0.0, 1.0).astype(jnp.float32)
    weights = jnp.exp(concentration * cosine) * keep_mask[:, :, None]
    spectral = jnp.dot(
        weights.reshape(row_count * row_count, -1),
        backward,
        precision=highest,
        preferred_element_type=jnp.float32,
    ).reshape(row_count, row_count, -1)
    degree = jnp.sum(spectral[:, :, 0], axis=1)
    rounded = spectral.astype(jnp.bfloat16)
    weight_real = jnp.concatenate([rounded[:, :, :half_width], rounded[:, :, :half_width]], axis=2)
    weight_imag = jnp.concatenate([-rounded[:, :, half_width:], rounded[:, :, half_width:]], axis=2)
    filtered = jnp.einsum(
        "ijc,jrc->irc", weight_real, other_block, preferred_element_type=jnp.float32
    )
    filtered = filtered + jnp.einsum(
        "ijc,jrc->irc", weight_imag, swapped, preferred_element_type=jnp.float32
    )
    return (filtered, degree)


def body(coefficients):
    own_block = lax.all_gather(coefficients, "off", axis=1, tiled=True)
    own_inverse = inverse_norms(own_block)
    row_count, radial, angular = own_block.shape
    forward, backward = angle_tables(angular)
    ranges = lax.axis_size("off")
    per_range = min(8, lax.axis_size("blk") // ranges)
    range_index = lax.axis_index("off")
    range_base = range_index * per_range
    packet = own_block
    packet = shifted(packet, "blk", -(per_range // 2))
    for bit_number in range(ranges.bit_length() - 1):
        moved_packet = shifted(packet, "blk", -(per_range << bit_number))
        chosen = range_index // (1 << bit_number) % 2 == 1
        packet = jnp.where(chosen, moved_packet, packet)
    empty_sum = jnp.zeros((row_count, radial, angular), jnp.float32)
    empty_degree = jnp.zeros((row_count,), jnp.float32)
    centre = range_base + per_range // 2
    lower_block = shifted(packet, "blk", 1)

    def advance_both(step, loop_state):
        filtered, degree, upper_block, lower_part = loop_state
        upper_terms = tile_terms(
            own_block, own_inverse, upper_block, centre + step, forward, backward
        )
        lower_terms = tile_terms(
            own_block, own_inverse, lower_part, centre - 1 - step, forward, backward
        )
        upper_block = shifted(upper_block, "blk", -1)
        lower_part = shifted(lower_part, "blk", 1)
        return (
            filtered + upper_terms[0] + lower_terms[0],
            degree + upper_terms[1] + lower_terms[1],
            upper_block,
            lower_part,
        )

    last_step = per_range // 2 - 1
    filtered, degree, upper_block, lower_block = lax.fori_loop(
        0, last_step, advance_both, (empty_sum, empty_degree, packet, lower_block)
    )
    upper_terms = tile_terms(
        own_block, own_inverse, upper_block, centre + last_step, forward, backward
    )
    lower_terms = tile_terms(
        own_block, own_inverse, lower_block, centre - 1 - last_step, forward, backward
    )
    filtered = filtered + upper_terms[0] + lower_terms[0]
    degree = degree + upper_terms[1] + lower_terms[1]
    totals = (
        lax.psum_scatter(filtered, "off", scatter_dimension=0, tiled=True),
        lax.psum_scatter(degree, "off", scatter_dimension=0, tiled=True),
    )
    smoothed = totals[0] / totals[1][:, None, None]
    return (smoothed, jnp.log(totals[1]))


def solution(mesh):
    return jax.shard_map(
        body,
        mesh=mesh,
        in_specs=(P("blk", "off", None),),
        out_specs=(P(("blk", "off"), None, None), P(("blk", "off"))),
        check_vma=False,
    )
```

profile of v0, /device:TPU:0, one launch (start us, length us, event | category | flops | bytes accessed | tf_op | source)
XLA Modules:
  0.0 91.2 jit_solution(6162711789580707457)
XLA Ops:
  7.2 1.0 %copy.17 = bf16[16,8,128]{0,1,2:T(8,128)(2,1)S(1)} copy(bf16[16,8,128]{2,1,0:T(8,128)(2,1)} %param.1) | data formatting | bytes 65536 | tf_op args[0]
  8.2 23.4 %all_gather.3 = bf16[16,32,128]{0,1,2:T(8,128)(2,1)S(1)} all-gather(bf16[16,8,128]{0,1,2:T(8,128)(2,1)S(1)} %copy.17), channel_id=1, replica_groups=mesh['blk'=8,'off'=4] {'off'}, dimensions={1}, use_global_device_ids=true | all-gather | bytes 163840 | tf_op jit(solution)/shard_map/all_gather | solution.py:74
  31.6 1.2 %copy.18 = bf16[16,32,128]{2,1,0:T(8,128)(2,1)S(1)} copy(bf16[16,32,128]{0,1,2:T(8,128)(2,1)S(1)} %all_gather.3) | data formatting | bytes 262144 | tf_op jit(solution)/shard_map/all_gather | solution.py:74
  32.8 1.2 %collective-permute-start = (bf16[16,32,128]{2,1,0:T(8,128)(2,1)S(1)}, bf16[16,32,128]{2,1,0:T(8,128)(2,1)S(1)}, u32[]{:S(2)}, u32[]{:S(2)}) collective-permute-start(bf16[16,32,128]{2,1,0:T(8,128)(2,1)S(1)} %copy.18), channel_id=1, source_target_pairs={{0,28},{4,0},{8,4},{12,8},{16,12},{20,16},{24,20},{28,24},{1,29},{... | collective-permute-start | bytes 393224 | tf_op jit(solution)/shard_map/ppermute | solution.py:13
  34.0 0.6 multiply_reduce_fusion
  34.5 2.0 %collective-permute-done = bf16[16,32,128]{2,1,0:T(8,128)(2,1)S(1)} collective-permute-done((bf16[16,32,128]{2,1,0:T(8,128)(2,1)S(1)}, bf16[16,32,128]{2,1,0:T(8,128)(2,1)S(1)}, u32[]{:S(2)}, u32[]{:S(2)}) %collective-permute-start) | collective-permute-done | bytes 131104 | tf_op jit(solution)/shard_map/ppermute | solution.py:13
  36.5 1.3 %collective-permute-start.1 = (bf16[16,32,128]{2,1,0:T(8,128)(2,1)S(1)}, bf16[16,32,128]{2,1,0:T(8,128)(2,1)S(1)}, u32[]{:S(2)}, u32[]{:S(2)}) collective-permute-start(bf16[16,32,128]{2,1,0:T(8,128)(2,1)S(1)} %collective-permute-done), channel_id=1, source_target_pairs={{0,24},{4,28},{8,0},{12,4},{16,8},{20,12},{24,16},{28,20},{1,25},{... | collective-permute-start | bytes 393224 | tf_op jit(solution)/shard_map/ppermute | solution.py:13
  37.9 4.7 %collective-permute-done.1 = bf16[16,32,128]{2,1,0:T(8,128)(2,1)S(1)} collective-permute-done((bf16[16,32,128]{2,1,0:T(8,128)(2,1)S(1)}, bf16[16,32,128]{2,1,0:T(8,128)(2,1)S(1)}, u32[]{:S(2)}, u32[]{:S(2)}) %collective-permute-start.1) | collective-permute-done | bytes 131104 | tf_op jit(solution)/shard_map/ppermute | solution.py:13
  42.5 0.3 collective-permute-start.2
  42.9 0.1 sine_negate_fusion
  43.0 4.8 %collective-permute-done.2 = bf16[16,32,128]{2,1,0:T(8,128)(2,1)S(1)} collective-permute-done((bf16[16,32,128]{2,1,0:T(8,128)(2,1)S(1)}, bf16[16,32,128]{2,1,0:T(8,128)(2,1)S(1)}, u32[]{:S(2)}, u32[]{:S(2)}) %collective-permute-start.2) | collective-permute-done | bytes 131104 | tf_op jit(solution)/shard_map/ppermute | solution.py:13
  47.8 0.2 multiply_reduce_fusion.2
  48.0 0.2 collective-permute-start.3
  48.3 0.4 copy.23
  48.9 0.4 copy.20
  49.3 0.4 convolution_bitcast_fusion.2
  49.8 0.3 copy.22
  50.1 0.4 convolution_bitcast_fusion.3
  50.6 0.3 copy.21
  50.9 0.3 fusion.5
  51.2 0.3 fusion.39
  51.7 0.4 copy.26
  52.1 1.4 %fusion.40 = f32[128,32,16]{1,2,0:T(8,128)} fusion(bf16[16,16,128]{1,0,2:T(8,128)(2,1)S(1)} %copy.26, bf16[16,32,128]{1,0,2:T(8,128)(2,1)S(1)} %copy.20), kind=kOutput, calls=%fused_computation.77 | convolution fusion | flops 2097152 | bytes 458752 | tf_op jit(solution)/shard_map/ijc,jrc->irc/dot_general | solution.py:67
  53.6 1.2 %copy.24 = bf16[16,16,128]{1,0,2:T(8,128)(2,1)} copy(bf16[16,16,128]{2,1,0:T(8,128)(2,1)S(1)} %pad_maximum_fusion.2) | data formatting | bytes 131072 | tf_op jit(solution)/shard_map/concatenate | solution.py:62
  55.1 0.4 copy.28
  55.5 0.4 convolution_bitcast_fusion
  56.0 0.3 copy.30
  56.3 0.4 copy.31
  56.7 0.4 convolution_bitcast_fusion.1
  57.2 0.3 copy.29
  57.5 0.2 multiply_reduce_fusion.1
  57.7 0.3 fusion.9
  58.0 0.3 fusion.38
  58.5 0.4 copy.34
  58.9 0.4 fusion.41
  59.4 0.4 copy.32
  59.9 0.4 convolution_add_fusion
  60.3 0.8 copy-done
  61.1 0.1 copy-done.1
  61.2 0.4 fusion.1
  61.6 1.1 %copy.35 = f32[16,32,128]{2,1,0:T(8,128)} copy(f32[16,32,128]{1,0,2:T(8,128)S(1)} %fusion.1) | data formatting | bytes 524288 | tf_op jit(solution)/shard_map/add | solution.py:120
  62.8 0.6 dynamic-slice
  64.0 0.2 slice_reduce_fusion.1
  64.2 0.2 slice_reduce_fusion
  64.4 10.6 %all-reduce = f32[16]{0:T(128)S(1)} all-reduce(f32[16]{0:T(128)S(1)} %add.84), channel_id=3, replica_groups=mesh['blk'=8,'off'=4] {'off'}, use_global_device_ids=true, to_apply=%region_6.7.clone | all-reduce | flops 16 | bytes 128
  75.0 0.6 fusion.33
  75.6 7.2 %reduce-scatter.2.cloned.1.call-done = f32[4,32,128]{2,1,0:T(8,128)} async-done(((f32[16,32,128]{2,1,0:T(8,128)}), f32[4,32,128]{2,1,0:T(8,128)}) %reduce-scatter.2.cloned.1.call-update) | async-done | bytes 65552 | tf_op jit(solution)/shard_map/reduce_scatter | solution.py:123
  82.8 1.5 %broadcast_divide_fusion = f32[4,32,128]{2,1,0:T(8,128)} fusion(f32[4,32,128]{2,1,0:T(8,128)} %reduce-scatter.2.cloned.1.call-done, f32[4]{0:T(128)S(1)} %get-tuple-element.5), kind=kLoop, calls=%fused_computation.48 | loop fusion | flops 16384 | bytes 131088 | tf_op jit(solution)/shard_map/div | solution.py:126
  (28 shorter events, 1.4 us)
Async XLA Ops:
  7.2 75.7 %reduce-scatter.2.cloned.1.call-start = ((), (), s32[]{:S(2)}) async-start(), calls=%async_computation.1 | async-start | bytes 327680 | tf_op jit(solution)/shard_map/reduce_scatter | solution.py:123
  32.8 3.7 %collective-permute-start = (bf16[16,32,128]{2,1,0:T(8,128)(2,1)S(1)}, bf16[16,32,128]{2,1,0:T(8,128)(2,1)S(1)}, u32[]{:S(2)}, u32[]{:S(2)}) collective-permute-start(bf16[16,32,128]{2,1,0:T(8,128)(2,1)S(1)} %copy.18), channel_id=1, source_target_pairs={{0,28},{4,0},{8,4},{12,8},{16,12},{20,16},{24,20},{28,24},{1,29},{... | collective-permute-start | bytes 393224 | tf_op jit(solution)/shard_map/ppermute | solution.py:13
  36.5 6.0 %collective-permute-start.1 = (bf16[16,32,128]{2,1,0:T(8,128)(2,1)S(1)}, bf16[16,32,128]{2,1,0:T(8,128)(2,1)S(1)}, u32[]{:S(2)}, u32[]{:S(2)}) collective-permute-start(bf16[16,32,128]{2,1,0:T(8,128)(2,1)S(1)} %collective-permute-done), channel_id=1, source_target_pairs={{0,24},{4,28},{8,0},{12,4},{16,8},{20,12},{24,16},{28,20},{1,25},{... | collective-permute-start | bytes 393224 | tf_op jit(solution)/shard_map/ppermute | solution.py:13
  42.5 5.2 %collective-permute-start.2 = (bf16[16,32,128]{2,1,0:T(8,128)(2,1)S(1)}, bf16[16,32,128]{2,1,0:T(8,128)(2,1)S(1)}, u32[]{:S(2)}, u32[]{:S(2)}) collective-permute-start(bf16[16,32,128]{2,1,0:T(8,128)(2,1)S(1)} %broadcast_select_fusion), channel_id=1, source_target_pairs={{0,16},{4,20},{8,24},{12,28},{16,0},{20,4},{24,8},{28,12},{1,17},{... | collective-permute-start | bytes 393224 | tf_op jit(solution)/shard_map/ppermute | solution.py:13
  48.0 6.8 %collective-permute-start.3 = (bf16[16,32,128]{2,1,0:T(8,128)(2,1)S(1)}, bf16[16,32,128]{2,1,0:T(8,128)(2,1)S(1)}, u32[]{:S(2)}, u32[]{:S(2)}) collective-permute-start(bf16[16,32,128]{2,1,0:T(8,128)(2,1)S(1)} %get-tuple-element.7), channel_id=1, source_target_pairs={{0,4},{4,8},{8,12},{12,16},{16,20},{20,24},{24,28},{28,0},{1,5},{5... | collective-permute-start | bytes 393224 | tf_op jit(solution)/shard_map/ppermute | solution.py:13
  59.9 1.2 %copy-start = (f32[128,32,16]{1,2,0:T(8,128)S(1)}, f32[128,32,16]{1,2,0:T(8,128)}, u32[]{:S(2)}) copy-start(f32[128,32,16]{1,2,0:T(8,128)} %fusion.40) | copy-start | bytes 786436
  59.9 1.3 %copy-start.1 = (bf16[16,16,128]{1,0,2:T(8,128)(2,1)S(1)}, bf16[16,16,128]{1,0,2:T(8,128)(2,1)}, u32[]{:S(2)}) copy-start(bf16[16,16,128]{1,0,2:T(8,128)(2,1)} %copy.24) | copy-start | bytes 196612
  61.6 1.2 %copy-start.2 = (u32[32]{0:T(128)S(1)}, u32[32]{0:T(128)}, u32[]{:S(2)}) copy-start(u32[32]{0:T(128)} %constant.70) | copy-start | bytes 388
Sparse Core Ops, SparseCore 0:
  62.9 19.8 reduce-scatter.1
where the time goes:
time: 91.5 us; the launch traced here: 91.2 us
  blocking collectives  34 us (37%)
  waiting for transfers between devices  18.7 us (20%)
  between operations  15 us (16%)
  local copies, waits for them, and re-layouts  10.9 us (12%)
  matrix products  5.46 us (6%)
  other arithmetic  4.18 us (5%)
  starting transfers between devices  3.05 us (3%)
    all_gather x1, blocking collectives, body(): own_block = lax.all_gather(coefficients, 'off', axis=1, tiled=True)  23.4 us
    ppermute x4, waiting for transfers between devices, shifted(): lax.ppermute(array, axis, [(i, (i + by) % count) for i in range(count)])  11.4 us
    unnamed x1, blocking collectives  10.6 us
    reduce_scatter x1, waiting for transfers between devices, body(): lax.psum_scatter(filtered, 'off', scatter_dimension=0, tiled=True)  7.22 us
    ppermute x4, starting transfers between devices, shifted(): lax.ppermute(array, axis, [(i, (i + by) % count) for i in range(count)])  3.02 us
    unnamed x8, local copies, waits for them, and re-layouts  2.54 us
  transfers between devices with their start and end apart: 5, of which 4 were waited for; matrix products, arithmetic and copies ran while one was open for 10% of the time, Pallas kernels for 0%

commit v1 on v0

--- a/solution.py
+++ b/solution.py
@@ -71,7 +71,12 @@
 
 
 def body(coefficients):
-    own_block = lax.all_gather(coefficients, "off", axis=1, tiled=True)
+    ring = [coefficients]
+    for hop in range(3):
+        ring.append(lax.ppermute(ring[-1], "off", [(dev, (dev + 1) % 4) for dev in range(4)]))
+    own_block = jnp.roll(
+        jnp.concatenate(ring[::-1], axis=1), (lax.axis_index("off") + 1) * ring[0].shape[1], axis=1
+    )
     own_inverse = inverse_norms(own_block)
     row_count, radial, angular = own_block.shape
     forward, backward = angle_tables(angular)

time: 91.5 us -> 139 us (1.52)
  waiting for transfers between devices: 18.7 us -> 82.8 us
  blocking collectives: 34 us -> 8.53 us
  local copies, waits for them, and re-layouts: 10.9 us -> 16 us
  starting transfers between devices: 3.05 us -> 5.8 us
  other arithmetic: 4.18 us -> 5.66 us
    ppermute x0 -> x3, waiting for transfers between devices: none -> 42.8 us  [body(): lax.ppermute(ring[-1], 'off', [(dev, (dev + 1) % 4) for dev in range(4)])]
    all_gather x1 -> x0, blocking collectives: 23.4 us -> none  [body(): own_block = lax.all_gather(coefficients, 'off', axis=1, tiled=True)]
    ppermute x4, waiting for transfers between devices: 11.4 us -> 32.9 us  [shifted(): lax.ppermute(array, axis, [(i, (i + by) % count) for i in range(count)])]
    concatenate x2 -> x1, local copies, waits for them, and re-layouts: 0.86 us -> 5.3 us  [body(): jnp.roll(jnp.concatenate(ring[::-1], axis=1), (lax.axis_index('off') + 1)...]
    ppermute x0 -> x3, starting transfers between devices: none -> 3.08 us  [body(): lax.ppermute(ring[-1], 'off', [(dev, (dev + 1) % 4) for dev in range(4)])]
    unnamed x1, blocking collectives: 10.6 us -> 8.53 us
  transfers between devices with their start and end apart: 5 -> 8, of which waited for: 4 -> 8; matrix products, arithmetic and copies ran while one was open for 10% -> 8% of each run, Pallas kernels for 0% -> 0%
where the time goes in v1:
time: 139 us
  waiting for transfers between devices  82.8 us (60%)
  local copies, waits for them, and re-layouts  16 us (12%)
  between operations  14.9 us (11%)
  blocking collectives  8.53 us (6%)
  starting transfers between devices  5.8 us (4%)
  other arithmetic  5.66 us (4%)
  matrix products  5.34 us (4%)
    ppermute x3, waiting for transfers between devices, body(): lax.ppermute(ring[-1], 'off', [(dev, (dev + 1) % 4) for dev in range(4)])  42.8 us
    ppermute x4, waiting for transfers between devices, shifted(): lax.ppermute(array, axis, [(i, (i + by) % count) for i in range(count)])  32.9 us
    unnamed x1, blocking collectives  8.53 us
    reduce_scatter x1, waiting for transfers between devices, body(): lax.psum_scatter(filtered, 'off', scatter_dimension=0, tiled=True)  7.04 us
    concatenate x1, local copies, waits for them, and re-layouts, body(): jnp.roll(jnp.concatenate(ring[::-1], axis=1), (lax.axis_index('off') + 1)...  5.3 us
    unnamed x8, local copies, waits for them, and re-layouts  3.35 us
    ppermute x3, starting transfers between devices, body(): lax.ppermute(ring[-1], 'off', [(dev, (dev + 1) % 4) for dev in range(4)])  3.08 us
  transfers between devices with their start and end apart: 8, of which 8 were waited for; matrix products, arithmetic and copies ran while one was open for 8% of the time, Pallas kernels for 0%

profile of v1, /device:TPU:0, one launch (start us, length us, event | category | flops | bytes accessed | tf_op | source)
XLA Modules:
  0.0 139.0 jit_solution(1105108783790848639)
XLA Ops:
  7.2 1.2 copy.31
  8.4 3.1 %collective-permute-start = (bf16[16,8,128]{1,0,2:T(8,128)(2,1)S(1)}, bf16[16,8,128]{1,0,2:T(8,128)(2,1)S(1)}, u32[]{:S(2)}, u32[]{:S(2)}) collective-permute-start(bf16[16,8,128]{1,0,2:T(8,128)(2,1)S(1)} %copy.31), channel_id=1, source_target_pairs={{0,1},{1,2},{2,3},{3,0},{4,5},{5,6},{6,7},{7,4},{8,9},{9,10},{10,1... | collective-permute-start | bytes 98312 | tf_op jit(solution)/shard_map/ppermute | solution.py:76
  11.5 13.9 %collective-permute-done = bf16[16,8,128]{1,0,2:T(8,128)(2,1)S(1)} collective-permute-done((bf16[16,8,128]{1,0,2:T(8,128)(2,1)S(1)}, bf16[16,8,128]{1,0,2:T(8,128)(2,1)S(1)}, u32[]{:S(2)}, u32[]{:S(2)}) %collective-permute-start) | collective-permute-done | bytes 32800 | tf_op jit(solution)/shard_map/ppermute | solution.py:76
  25.4 14.9 %collective-permute-done.1 = bf16[16,8,128]{1,0,2:T(8,128)(2,1)S(1)} collective-permute-done((bf16[16,8,128]{1,0,2:T(8,128)(2,1)S(1)}, bf16[16,8,128]{1,0,2:T(8,128)(2,1)S(1)}, u32[]{:S(2)}, u32[]{:S(2)}) %collective-permute-start.1) | collective-permute-done | bytes 32800 | tf_op jit(solution)/shard_map/ppermute | solution.py:76
  40.3 14.0 %collective-permute-done.2 = bf16[16,8,128]{1,0,2:T(8,128)(2,1)S(1)} collective-permute-done((bf16[16,8,128]{1,0,2:T(8,128)(2,1)S(1)}, bf16[16,8,128]{1,0,2:T(8,128)(2,1)S(1)}, u32[]{:S(2)}, u32[]{:S(2)}) %collective-permute-start.2) | collective-permute-done | bytes 32800 | tf_op jit(solution)/shard_map/ppermute | solution.py:76
  54.3 5.3 %concatenate.33 = bf16[16,64,128]{1,0,2:T(8,128)(2,1)S(1)} concatenate(bf16[16,8,128]{1,0,2:T(8,128)(2,1)S(1)} %collective-permute-done.2, bf16[16,8,128]{1,0,2:T(8,128)(2,1)S(1)} %collective-permute-done.1, bf16[16,8,128]{1,0,2:T(8,128)(2,1)S(1)} %collective-permute-done, bf16[16,8,128]{1,0,2:T(8,128)(2,1)S(1)} %copy.31, bf16[16,8,128]{1,0,2:T(8,128)(2,1)S(1)} %collective-permute-done.2, ...), dimensions={1} | concatenate | bytes 524288 | tf_op jit(solution)/shard_map/jit(_roll_dynamic)/concatenate | solution.py:77
  59.6 0.4 multiply_reduce_fusion.2
  60.1 6.7 %collective-permute-done.3 = bf16[16,32,128]{1,0,2:T(8,128)(2,1)S(1)} collective-permute-done((bf16[16,32,128]{1,0,2:T(8,128)(2,1)S(1)}, bf16[16,32,128]{1,0,2:T(8,128)(2,1)S(1)}, u32[]{:S(2)}, u32[]{:S(2)}) %collective-permute-start.3) | collective-permute-done | bytes 131104 | tf_op jit(solution)/shard_map/ppermute | solution.py:13
  66.8 2.0 %collective-permute-start.4 = (bf16[16,32,128]{1,0,2:T(8,128)(2,1)S(1)}, bf16[16,32,128]{1,0,2:T(8,128)(2,1)S(1)}, u32[]{:S(2)}, u32[]{:S(2)}) collective-permute-start(bf16[16,32,128]{1,0,2:T(8,128)(2,1)S(1)} %collective-permute-done.3), channel_id=1, source_target_pairs={{0,24},{4,28},{8,0},{12,4},{16,8},{20,12},{24,16},{28,20},{1,25},{... | collective-permute-start | bytes 393224 | tf_op jit(solution)/shard_map/ppermute | solution.py:13
  68.7 0.1 sine_negate_fusion
  68.9 12.4 %collective-permute-done.4 = bf16[16,32,128]{1,0,2:T(8,128)(2,1)S(1)} collective-permute-done((bf16[16,32,128]{1,0,2:T(8,128)(2,1)S(1)}, bf16[16,32,128]{1,0,2:T(8,128)(2,1)S(1)}, u32[]{:S(2)}, u32[]{:S(2)}) %collective-permute-start.4) | collective-permute-done | bytes 131104 | tf_op jit(solution)/shard_map/ppermute | solution.py:13
  81.3 0.6 collective-permute-start.5
  81.9 13.4 %collective-permute-done.5 = bf16[16,32,128]{1,0,2:T(8,128)(2,1)S(1)} collective-permute-done((bf16[16,32,128]{1,0,2:T(8,128)(2,1)S(1)}, bf16[16,32,128]{1,0,2:T(8,128)(2,1)S(1)}, u32[]{:S(2)}, u32[]{:S(2)}) %collective-permute-start.5) | collective-permute-done | bytes 131104 | tf_op jit(solution)/shard_map/ppermute | solution.py:13
  95.3 0.4 multiply_reduce_fusion.1
  95.8 0.4 convolution_bitcast_fusion.3
  96.2 0.4 convolution_bitcast_fusion.2
  96.6 0.9 slice_subtract_fusion.1
  97.4 1.3 copy.35
  98.7 0.9 slice_add_fusion.1
  99.6 1.3 copy.34
  100.9 0.3 fusion.5
  101.2 0.3 fusion.45
  101.7 0.4 copy.37
  102.2 1.4 fusion.11
  103.6 1.2 copy.36
  104.8 0.4 collective-permute-done.6
  105.3 0.4 convolution_bitcast_fusion
  105.7 0.3 copy.39
  106.0 0.4 convolution_bitcast_fusion.1
  106.5 0.3 copy.38
  106.8 0.3 multiply_reduce_fusion
  107.1 0.3 fusion.9
  107.4 0.3 fusion.44
  107.9 0.4 copy.41
  108.3 0.4 fusion.10
  108.8 0.4 copy.40
  109.3 0.4 convolution_add_fusion
  109.7 0.8 copy-done
  110.6 0.4 fusion.1
  111.0 1.1 copy.42
  112.2 0.6 copy-done.2
  112.8 0.6 dynamic-slice
  114.0 0.2 slice_reduce_fusion.1
  114.2 0.2 slice_reduce_fusion
  114.5 8.5 %all-reduce = f32[16]{0:T(128)S(1)} all-reduce(f32[16]{0:T(128)S(1)} %add.100), channel_id=3, replica_groups=mesh['blk'=8,'off'=4] {'off'}, use_global_device_ids=true, to_apply=%region_6.7.clone | all-reduce | flops 16 | bytes 128
  123.0 0.6 fusion.39
  123.6 7.0 %reduce-scatter.2.cloned.1.call-done = f32[4,32,128]{2,1,0:T(8,128)} async-done(((f32[16,32,128]{2,1,0:T(8,128)}), f32[4,32,128]{2,1,0:T(8,128)}) %reduce-scatter.2.cloned.1.call-update) | async-done | bytes 65552 | tf_op jit(solution)/shard_map/reduce_scatter | solution.py:128
  130.6 1.5 %broadcast_divide_fusion = f32[4,32,128]{2,1,0:T(8,128)} fusion(f32[4,32,128]{2,1,0:T(8,128)} %reduce-scatter.2.cloned.1.call-done, f32[4]{0:T(128)S(1)} %get-tuple-element.5), kind=kLoop, calls=%fused_computation.50 | loop fusion | flops 16384 | bytes 131088 | tf_op jit(solution)/shard_map/div | solution.py:131
  (27 shorter events, 1.2 us)
Async XLA Ops:
  7.2 123.5 %reduce-scatter.2.cloned.1.call-start = ((), (), s32[]{:S(2)}) async-start(), calls=%async_computation.1 | async-start | bytes 327680 | tf_op jit(solution)/shard_map/reduce_scatter | solution.py:128
  8.4 17.0 %collective-permute-start = (bf16[16,8,128]{1,0,2:T(8,128)(2,1)S(1)}, bf16[16,8,128]{1,0,2:T(8,128)(2,1)S(1)}, u32[]{:S(2)}, u32[]{:S(2)}) collective-permute-start(bf16[16,8,128]{1,0,2:T(8,128)(2,1)S(1)} %copy.31), channel_id=1, source_target_pairs={{0,1},{1,2},{2,3},{3,0},{4,5},{5,6},{6,7},{7,4},{8,9},{9,10},{10,1... | collective-permute-start | bytes 98312 | tf_op jit(solution)/shard_map/ppermute | solution.py:76
  25.4 14.9 %collective-permute-start.1 = (bf16[16,8,128]{1,0,2:T(8,128)(2,1)S(1)}, bf16[16,8,128]{1,0,2:T(8,128)(2,1)S(1)}, u32[]{:S(2)}, u32[]{:S(2)}) collective-permute-start(bf16[16,8,128]{1,0,2:T(8,128)(2,1)S(1)} %collective-permute-done), channel_id=1, source_target_pairs={{0,1},{1,2},{2,3},{3,0},{4,5},{5,6},{6,7},{7,4},{8,9},{9,10},{10,1... | collective-permute-start | bytes 98312 | tf_op jit(solution)/shard_map/ppermute | solution.py:76
  40.3 14.0 %collective-permute-start.2 = (bf16[16,8,128]{1,0,2:T(8,128)(2,1)S(1)}, bf16[16,8,128]{1,0,2:T(8,128)(2,1)S(1)}, u32[]{:S(2)}, u32[]{:S(2)}) collective-permute-start(bf16[16,8,128]{1,0,2:T(8,128)(2,1)S(1)} %collective-permute-done.1), channel_id=1, source_target_pairs={{0,1},{1,2},{2,3},{3,0},{4,5},{5,6},{6,7},{7,4},{8,9},{9,10},{10,1... | collective-permute-start | bytes 98312 | tf_op jit(solution)/shard_map/ppermute | solution.py:76
  60.0 6.8 %collective-permute-start.3 = (bf16[16,32,128]{1,0,2:T(8,128)(2,1)S(1)}, bf16[16,32,128]{1,0,2:T(8,128)(2,1)S(1)}, u32[]{:S(2)}, u32[]{:S(2)}) collective-permute-start(bf16[16,32,128]{1,0,2:T(8,128)(2,1)S(1)} %get-tuple-element.9), channel_id=1, source_target_pairs={{0,28},{4,0},{8,4},{12,8},{16,12},{20,16},{24,20},{28,24},{1,29},{... | collective-permute-start | bytes 393224 | tf_op jit(solution)/shard_map/ppermute | solution.py:13
  66.8 14.5 %collective-permute-start.4 = (bf16[16,32,128]{1,0,2:T(8,128)(2,1)S(1)}, bf16[16,32,128]{1,0,2:T(8,128)(2,1)S(1)}, u32[]{:S(2)}, u32[]{:S(2)}) collective-permute-start(bf16[16,32,128]{1,0,2:T(8,128)(2,1)S(1)} %collective-permute-done.3), channel_id=1, source_target_pairs={{0,24},{4,28},{8,0},{12,4},{16,8},{20,12},{24,16},{28,20},{1,25},{... | collective-permute-start | bytes 393224 | tf_op jit(solution)/shard_map/ppermute | solution.py:13
  81.3 14.0 %collective-permute-start.5 = (bf16[16,32,128]{1,0,2:T(8,128)(2,1)S(1)}, bf16[16,32,128]{1,0,2:T(8,128)(2,1)S(1)}, u32[]{:S(2)}, u32[]{:S(2)}) collective-permute-start(bf16[16,32,128]{1,0,2:T(8,128)(2,1)S(1)} %broadcast_select_fusion), channel_id=1, source_target_pairs={{0,16},{4,20},{8,24},{12,28},{16,0},{20,4},{24,8},{28,12},{1,17},{... | collective-permute-start | bytes 393224 | tf_op jit(solution)/shard_map/ppermute | solution.py:13
  95.7 9.6 %collective-permute-start.6 = (bf16[16,32,128]{1,0,2:T(8,128)(2,1)S(1)}, bf16[16,32,128]{1,0,2:T(8,128)(2,1)S(1)}, u32[]{:S(2)}, u32[]{:S(2)}) collective-permute-start(bf16[16,32,128]{1,0,2:T(8,128)(2,1)S(1)} %get-tuple-element.7), channel_id=1, source_target_pairs={{0,4},{4,8},{8,12},{12,16},{16,20},{20,24},{24,28},{28,0},{1,5},{5... | collective-permute-start | bytes 393224 | tf_op jit(solution)/shard_map/ppermute | solution.py:13
  109.2 1.2 copy-start
  109.3 1.3 copy-start.1
  112.1 0.7 copy-start.2
Sparse Core Ops, SparseCore 0:
  112.3 18.3 reduce-scatter.1
